TPU v7x, 32 devices: a whole 2x2x4 slice. The times are simulated.
32 devices in a mesh: curve: 16 (over z, x, core), group: 2 (over y).
Axes of the slice: x: 2, y: 2, z: 4, core: 2. Of those that a mesh axis runs over, the one named last changes fastest.
Arguments:
- field: float32 [3, 256, 64, 128], P(None, 'curve', 'group'), may hold values from -6 to 6
- source: float32 [3, 256, 64, 128], P(None, 'curve', 'group'), may hold values from -16 to 16
- mass: float32 [256, 64, 128], P('curve', 'group'), may hold values from 0.5 to 8
- interp: float32 [4, 128, 128], replicated, may hold values from -0.5 to 1.5
- parent_list: int32 [16, 2, 2, 16], P('curve', 'group'), may hold values from 0 to 511
- child_list: int32 [16, 2, 2, 16], P('curve', 'group'), may hold values from 0 to 511
- child_kind: int32 [16, 2, 2, 16], P('curve', 'group'), may hold values from 0 to 3
- counts: int32 [16, 2, 2], P('curve', 'group'), may hold values from 0 to 16, as said below
Outputs:
- cycle: float32 [3, 256, 64, 128], P(None, 'curve', 'group')
Inputs may be any that keep to these rules, and one draw needn't show every extreme that they name: `parent_list`: local block index x * 32 + y on the device that owns the parent. `child_list`: local block index x * 32 + y on the device that owns the child. `counts`: in every draw, in each curve segment one destination group receives 16 live slots from every source group; every other destination group receives at most 8 live slots from each source group.
All inputs are finite; a program needn't handle non-finite values.
Results may differ from a plain program's by a relative error of at most 0.0001.
Values sent between devices are 32-bit elements; how exact they have to be, the bound alone decides.
A program may use at most 64 MiB of HBM per device.

v0:
```python
import jax
import jax.numpy as jnp
from jax import lax
from jax.sharding import PartitionSpec as P

SWEEPS = 2


OMEGA = 2.0 / 3.0


def extended(cells, sides, width):
    for axis, dim in sides:
        count = lax.axis_size(axis)
        ends = count - 1
        head = lax.slice_in_dim(cells, 0, width, axis=dim)
        tail = lax.slice_in_dim(cells, cells.shape[dim] - width, cells.shape[dim], axis=dim)
        cells = jnp.concatenate(
            [
                lax.ppermute(tail, axis, [(i, (i + 1) % count) for i in range(ends)]),
                cells,
                lax.ppermute(head, axis, [((i + 1) % count, i) for i in range(ends)]),
            ],
            axis=dim,
        )
    return cells


def relax(padded, source, mass):
    centre = padded[:, 1:-1, 1:-1, :]
    beside = (
        padded[:, 2:, 1:-1, :]
        + padded[:, :-2, 1:-1, :]
        + padded[:, 1:-1, 2:, :]
        + padded[:, 1:-1, :-2, :]
    )
    z_pair = jnp.pad(centre, ((0, 0), (0, 0), (0, 0), (1, 1)))
    beside = beside + z_pair[..., 2:] + z_pair[..., :-2]
    diag_total = 6.0 + mass
    applied = diag_total * centre - beside
    return centre + OMEGA * (source - applied) / diag_total


def stacked(interp, order):
    kind_total = interp.shape[0]
    node_count = interp.shape[1]
    return jnp.transpose(interp, order).reshape(node_count, kind_total * node_count)


def pick_kind(product, onehot):
    return jnp.sum(product * onehot[None, :, :, :, None], axis=3)


def local(field, source, mass, interp, parent_list, child_list, child_kind, counts):
    components, rows_x, rows_y, node_count = field.shape
    groups = lax.axis_size("group")
    slot_count = parent_list.shape[3]
    kind_total = interp.shape[0]
    blocks = field.reshape(components, rows_x * rows_y, node_count)
    active = (jnp.arange(slot_count, dtype=jnp.int32)[None, :] < counts.reshape(groups, 1)).astype(
        jnp.float32
    )
    onehot = (
        child_kind.reshape(groups, slot_count, 1)
        == jnp.arange(kind_total, dtype=jnp.int32)[None, None, :]
    ).astype(jnp.float32)
    child_index = child_list.reshape(groups * slot_count)
    parent_index = parent_list.reshape(groups * slot_count)
    statics = extended(
        jnp.concatenate([source, mass[None]], axis=0), (("curve", 1), ("group", 2)), SWEEPS - 1
    )
    picked = (
        jnp.take(blocks, parent_index, axis=1).reshape(components, groups, slot_count, node_count)
        * active[None, :, :, None]
    )
    forward_table = stacked(interp, (1, 0, 2))
    arrived = lax.all_to_all(picked, "group", split_axis=1, concat_axis=1, tiled=True)
    shape = arrived.shape
    product = jnp.dot(
        arrived.reshape(-1, shape[3]),
        forward_table,
        precision=lax.Precision.HIGHEST,
        preferred_element_type=jnp.float32,
    )
    products = product.reshape(shape[0], shape[1], shape[2], kind_total, shape[3])
    hanging = pick_kind(products, onehot).reshape(components, groups * slot_count, node_count)
    constrained = (
        blocks.at[:, child_index].add(hanging).reshape(components, rows_x, rows_y, node_count)
    )
    padded = extended(constrained, (("curve", 1), ("group", 2)), SWEEPS)
    curve_start = lax.axis_index("curve") * rows_x
    group_start = lax.axis_index("group") * rows_y
    total_x = rows_x * lax.axis_size("curve")
    total_y = rows_y * groups
    for sweep_index in range(SWEEPS):
        margin = SWEEPS - 1 - sweep_index
        offset = SWEEPS - 1 - margin
        inner_source = statics[
            :3, offset : offset + rows_x + 2 * margin, offset : offset + rows_y + 2 * margin, :
        ]
        inner_mass = statics[
            3, offset : offset + rows_x + 2 * margin, offset : offset + rows_y + 2 * margin, :
        ]
        updated = relax(padded, inner_source, inner_mass)
        x_place = curve_start - margin + jnp.arange(rows_x + 2 * margin, dtype=jnp.int32)
        y_place = group_start - margin + jnp.arange(rows_y + 2 * margin, dtype=jnp.int32)
        inside = ((x_place >= 0) & (x_place < total_x))[:, None] & (
            (y_place >= 0) & (y_place < total_y)
        )[None, :]
        padded = updated * inside[None, :, :, None].astype(jnp.float32)
    correction = (padded - constrained).reshape(components, rows_x * rows_y, node_count)
    back_table = stacked(interp, (2, 0, 1))
    chosen = jnp.take(correction, child_index, axis=1)
    product = jnp.dot(
        chosen.reshape(-1, node_count),
        back_table,
        precision=lax.Precision.HIGHEST,
        preferred_element_type=jnp.float32,
    )
    restricted = pick_kind(
        product.reshape(components, groups, slot_count, kind_total, node_count), onehot
    )
    arrived = lax.all_to_all(restricted, "group", split_axis=1, concat_axis=1, tiled=True)
    arrived = arrived * active[None, :, :, None]
    summed = (
        jnp.zeros_like(blocks)
        .at[:, parent_index]
        .add(arrived.reshape(components, groups * slot_count, node_count))
    )
    return padded + summed.reshape(components, rows_x, rows_y, node_count)


def solution(mesh):
    in_specs = (
        P(None, "curve", "group", None),
        P(None, "curve", "group", None),
        P("curve", "group", None),
        P(),
        P("curve", "group", None, None),
        P("curve", "group", None, None),
        P("curve", "group", None, None),
        P("curve", "group", None),
    )
    out_specs = P(None, "curve", "group", None)
    return jax.shard_map(local, mesh=mesh, in_specs=in_specs, out_specs=out_specs, check_vma=False)
```

profile of v0, /device:TPU:8, one launch (start us, length us, event | category | flops | bytes accessed | tf_op | source)
XLA Modules:
  0.0 56.8 jit_solution(16389338205775795244)
XLA Ops:
  0.0 0.8 %reshape.237 = s32[32]{0:T(128)S(1)} reshape(s32[1,1,2,16]{3,2,1,0:T(2,128)} %param.14) | data formatting | bytes 256 | tf_op jit(solution)/shard_map/reshape | solution.py:68
  0.8 0.8 %reshape.244 = s32[32]{0:T(128)S(1)} reshape(s32[1,1,2,16]{3,2,1,0:T(2,128)} %param.15) | data formatting | bytes 256 | tf_op jit(solution)/shard_map/reshape | solution.py:67
  1.6 1.8 %copy.55 = f32[3,16,32,128]{3,0,2,1:T(4,128)S(1)} copy(f32[3,16,32,128]{3,2,1,0:T(8,128)} %param.10) | data formatting | bytes 1572864 | tf_op args[0]
  3.4 0.1 compare_convert_fusion
  3.4 0.6 %gather_fusion = f32[32,3,128]{2,1,0:T(4,128)S(1)} fusion(f32[3,512,128]{2,0,1:T(4,128)S(1)} %bitcast.57, s32[1024]{0:T(1024)S(1)} %get-tuple-element.17), kind=kCustom, calls=%fused_computation.clone | custom fusion | bytes 98432 | tf_op jit(solution)/shard_map/jit(_take)/gather | solution.py:73
  4.1 0.1 broadcast_select_fusion.1
  4.2 0.1 copy_multiply_fusion.1
  4.3 0.6 %copy.57 = f32[3,2,16,128]{3,2,0,1:T(8,128)} copy(f32[3,2,16,128]{3,2,1,0:T(8,128)S(1)} %copy_multiply_fusion.1) | data formatting | bytes 98304 | tf_op jit(solution)/shard_map/mul | solution.py:73
  4.9 3.3 %all-to-all-start = ((f32[3,2,16,128]{3,2,0,1:T(8,128)}), f32[3,2,16,128]{3,2,0,1:T(8,128)S(1)}, u32[]{:S(2)}, u32[]{:S(2)}) async-start(f32[3,2,16,128]{3,2,0,1:T(8,128)} %copy.57), calls=%async_computation | async-start | bytes 98304 | tf_op jit(solution)/shard_map/all_to_all | solution.py:77
  8.2 1.9 %collective-permute-start.4 = (f32[4,1,32,128]{3,2,1,0:T(8,128)S(1)}, f32[4,1,32,128]{3,2,1,0:T(8,128)S(1)}, u32[]{:S(2)}, u32[]{:S(2)}) collective-permute-start(f32[4,1,32,128]{3,2,1,0:T(8,128)S(1)} %get-tuple-element.10), channel_id=1, source_target_pairs={{0,2},{2,4},{4,6},{6,8},{8,10},{10,12},{12,14},{14,16},{16,18},{18... | collective-permute-start | bytes 196616 | tf_op jit(solution)/shard_map/ppermute | solution.py:20
  10.1 4.5 %collective-permute-start.5 = (f32[4,1,32,128]{3,2,1,0:T(8,128)S(1)}, f32[4,1,32,128]{3,2,1,0:T(8,128)S(1)}, u32[]{:S(2)}, u32[]{:S(2)}) collective-permute-start(f32[4,1,32,128]{3,2,1,0:T(8,128)S(1)} %get-tuple-element.11), channel_id=1, source_target_pairs={{2,0},{4,2},{6,4},{8,6},{10,8},{12,10},{14,12},{16,14},{18,16},{20... | collective-permute-start | bytes 196616 | tf_op jit(solution)/shard_map/ppermute | solution.py:22
  14.7 0.1 reshape.236
  14.9 0.1 and_convert_fusion
  15.0 0.1 and_convert_fusion.1
  15.0 0.1 reshape.242
  15.1 0.1 copy.58
  15.3 0.4 fusion
  15.7 1.6 %scatter_fusion = f32[3,512,128]{2,0,1:T(4,128)S(1)} fusion(f32[3,512,128]{2,0,1:T(4,128)S(1)} %bitcast.58, s32[32]{0:T(128)S(1)} %fusion.26, f32[32,3,128]{2,1,0:T(4,128)S(1)} %bitcast.69), kind=kCustom, calls=%fused_computation.2 | custom fusion | flops 12288 | bytes 147584 | tf_op jit(solution)/shard_map/scatter-add | solution.py:88
  17.4 0.1 copy.61
  17.5 3.9 %collective-permute-start.6 = (f32[4,18,1,128]{3,2,1,0:T(1,128)S(1)}, f32[4,18,1,128]{3,2,1,0:T(1,128)S(1)}, u32[]{:S(2)}, u32[]{:S(2)}) collective-permute-start(f32[4,18,1,128]{3,2,1,0:T(1,128)S(1)} %get-tuple-element.8), channel_id=1, source_target_pairs={{0,1},{2,3},{4,5},{6,7},{8,9},{10,11},{12,13},{14,15},{16,17},{18,... | collective-permute-start | bytes 110600 | tf_op jit(solution)/shard_map/ppermute | solution.py:20
  21.4 1.3 %collective-permute-start.7 = (f32[4,18,1,128]{3,2,1,0:T(1,128)S(1)}, f32[4,18,1,128]{3,2,1,0:T(1,128)S(1)}, u32[]{:S(2)}, u32[]{:S(2)}) collective-permute-start(f32[4,18,1,128]{3,2,1,0:T(1,128)S(1)} %get-tuple-element.9), channel_id=1, source_target_pairs={{1,0},{3,2},{5,4},{7,6},{9,8},{11,10},{13,12},{15,14},{17,16},{19,... | collective-permute-start | bytes 110600 | tf_op jit(solution)/shard_map/ppermute | solution.py:22
  22.8 1.9 %collective-permute-start = (f32[3,2,32,128]{3,2,1,0:T(8,128)S(1)}, f32[3,2,32,128]{3,2,1,0:T(8,128)S(1)}, u32[]{:S(2)}, u32[]{:S(2)}) collective-permute-start(f32[3,2,32,128]{3,2,1,0:T(8,128)S(1)} %get-tuple-element.15), channel_id=1, source_target_pairs={{0,2},{2,4},{4,6},{6,8},{8,10},{10,12},{12,14},{14,16},{16,18},{18... | collective-permute-start | bytes 294920 | tf_op jit(solution)/shard_map/ppermute | solution.py:20
  24.7 4.5 %collective-permute-start.1 = (f32[3,2,32,128]{3,2,1,0:T(8,128)S(1)}, f32[3,2,32,128]{3,2,1,0:T(8,128)S(1)}, u32[]{:S(2)}, u32[]{:S(2)}) collective-permute-start(f32[3,2,32,128]{3,2,1,0:T(8,128)S(1)} %get-tuple-element.14), channel_id=1, source_target_pairs={{2,0},{4,2},{6,4},{8,6},{10,8},{12,10},{14,12},{16,14},{18,16},{20... | collective-permute-start | bytes 294920 | tf_op jit(solution)/shard_map/ppermute | solution.py:22
  29.3 0.2 pad_maximum_fusion
  29.5 0.1 collective-permute-done
  29.6 0.1 constant_dynamic-update-slice_fusion.1
  29.7 1.7 %collective-permute-done.1 = f32[3,2,32,128]{3,2,1,0:T(8,128)S(1)} collective-permute-done((f32[3,2,32,128]{3,2,1,0:T(8,128)S(1)}, f32[3,2,32,128]{3,2,1,0:T(8,128)S(1)}, u32[]{:S(2)}, u32[]{:S(2)}) %collective-permute-start.1) | collective-permute-done | bytes 98336 | tf_op jit(solution)/shard_map/ppermute | solution.py:22
  31.5 4.5 %collective-permute-start.2 = (f32[3,20,2,128]{3,2,1,0:T(2,128)S(1)}, f32[3,20,2,128]{3,2,1,0:T(2,128)S(1)}, u32[]{:S(2)}, u32[]{:S(2)}) collective-permute-start(f32[3,20,2,128]{3,2,1,0:T(2,128)S(1)} %get-tuple-element.12), channel_id=1, source_target_pairs={{0,1},{2,3},{4,5},{6,7},{8,9},{10,11},{12,13},{14,15},{16,17},{18,... | collective-permute-start | bytes 184328 | tf_op jit(solution)/shard_map/ppermute | solution.py:20
  36.0 1.3 %collective-permute-start.3 = (f32[3,20,2,128]{3,2,1,0:T(2,128)S(1)}, f32[3,20,2,128]{3,2,1,0:T(2,128)S(1)}, u32[]{:S(2)}, u32[]{:S(2)}) collective-permute-start(f32[3,20,2,128]{3,2,1,0:T(2,128)S(1)} %get-tuple-element.13), channel_id=1, source_target_pairs={{1,0},{3,2},{5,4},{7,6},{9,8},{11,10},{13,12},{15,14},{17,16},{19,... | collective-permute-start | bytes 184328 | tf_op jit(solution)/shard_map/ppermute | solution.py:22
  37.3 0.1 fusion.20
  37.4 0.5 collective-permute-done.2
  37.9 4.3 %collective-permute-done.3 = f32[3,20,2,128]{3,2,1,0:T(2,128)S(1)} collective-permute-done((f32[3,20,2,128]{3,2,1,0:T(2,128)S(1)}, f32[3,20,2,128]{3,2,1,0:T(2,128)S(1)}, u32[]{:S(2)}, u32[]{:S(2)}) %collective-permute-start.3) | collective-permute-done | bytes 61472 | tf_op jit(solution)/shard_map/ppermute | solution.py:22
  42.2 0.2 pad_maximum_fusion.1
  42.4 0.1 slice.106
  42.5 0.9 %fusion.11 = f32[3,18,34,128]{3,2,1,0:T(8,128)S(1)} fusion(f32[3,18,34,128]{3,2,1,0:T(8,128)S(1)} %slice.106, f32[3,20,32,128]{3,2,1,0:T(8,128)S(1)} %constant_dynamic-update-slice_fusion, f32[3,20,2,128]{3,2,1,0:T(2,128)S(1)} %collective-permute-done.2, f32[3,20,2,128]{3,2,1,0:T(2,128)S(1)} %collective-permute-done.3, ...), kind=kLoop, calls=%fused_computation.26 | loop fusion | flops 3290112 | bytes 6121872 | tf_op jit(solution)/shard_map/mul | solution.py:110
  43.4 0.1 slice.110
  43.5 0.8 %fusion.28 = (f32[3,16,32,128]{3,2,1,0:T(8,128)S(1)}, f32[3,16,32,128]{3,2,1,0:T(8,128)S(1)}) fusion(f32[16,32]{1,0:T(8,128)S(1)} %and_convert_fusion.1, f32[3,16,32,128]{3,2,1,0:T(8,128)S(1)} %slice.110, f32[3,16,32,128]{3,2,1,0:T(8,128)S(1)} %copy-done, f32[3,18,34,128]{3,2,1,0:T(8,128)S(1)} %fusion.11, f32[16,32,128]{2,1,0:T(8,128)S(1)} %broadcast_add_fusion, ...), kind=kLoop, calls=%fused_computation.79 | loop fusion | flops 2555904 | bytes 7342080 | tf_op jit(solution)/shard_map/sub | solution.py:111
  44.3 0.5 copy.65
  44.8 0.6 %gather_fusion.1 = f32[32,3,128]{2,1,0:T(4,128)S(1)} fusion(f32[3,512,128]{2,0,1:T(4,128)S(1)} %bitcast.67, s32[1024]{0:T(1024)S(1)} %get-tuple-element.16), kind=kCustom, calls=%fused_computation.1.clone | custom fusion | bytes 98432 | tf_op jit(solution)/shard_map/jit(_take)/gather | solution.py:113
  45.4 0.1 broadcast_select_fusion
  45.5 0.4 fusion.1
  45.9 0.6 %copy.67 = f32[3,2,16,128]{3,2,0,1:T(8,128)} copy(f32[3,2,16,128]{3,2,1,0:T(8,128)S(1)} %fusion.1) | data formatting | bytes 98304 | tf_op jit(solution)/shard_map/reduce_sum | solution.py:51
  46.6 3.3 %all-to-all-start.1 = ((f32[3,2,16,128]{3,2,0,1:T(8,128)}), f32[3,2,16,128]{3,2,0,1:T(8,128)S(1)}, u32[]{:S(2)}, u32[]{:S(2)}) async-start(f32[3,2,16,128]{3,2,0,1:T(8,128)} %copy.67), calls=%async_computation.1 | async-start | bytes 98304 | tf_op jit(solution)/shard_map/all_to_all | solution.py:123
  49.9 4.0 %all-to-all-done.1 = f32[3,2,16,128]{3,2,0,1:T(8,128)S(1)} async-done(((f32[3,2,16,128]{3,2,0,1:T(8,128)}), f32[3,2,16,128]{3,2,0,1:T(8,128)S(1)}, u32[]{:S(2)}, u32[]{:S(2)}) %all-to-all-start.1) | async-done | bytes 49184 | tf_op jit(solution)/shard_map/all_to_all | solution.py:123
  53.9 0.1 copy_multiply_fusion
  54.0 0.1 broadcast_in_dim.14
  54.1 1.6 %scatter_fusion.1 = f32[3,512,128]{2,0,1:T(4,128)S(1)} fusion(f32[3,512,128]{2,0,1:T(4,128)S(1)} %broadcast_in_dim.14, s32[32]{0:T(128)S(1)} %fusion.27, f32[32,3,128]{2,1,0:T(4,128)S(1)} %copy.69), kind=kCustom, calls=%fused_computation.3 | custom fusion | flops 12288 | bytes 147584 | tf_op jit(solution)/shard_map/scatter-add | solution.py:128
  55.8 1.0 %copy_add_fusion = f32[3,16,32,128]{3,2,1,0:T(8,128)} fusion(f32[3,16,32,128]{3,2,1,0:T(8,128)S(1)} %get-tuple-element.7, f32[3,16,32,128]{3,0,2,1:T(4,128)S(1)} %bitcast.66), kind=kLoop, calls=%fused_computation.37 | loop fusion | flops 196608 | bytes 2359296 | tf_op jit(solution)/shard_map/add | solution.py:130
  (40 shorter events, 0.4 us)
Async XLA Ops:
  0.0 3.3 %copy-start.6 = (s32[1,1,2]{2,1,0:T(1,128)S(1)}, s32[1,1,2]{2,1,0:T(1,128)}, u32[]{:S(2)}) copy-start(s32[1,1,2]{2,1,0:T(1,128)} %param.17) | copy-start | bytes 28
  1.6 6.6 %copy-start = (f32[3,16,32,128]{3,2,1,0:T(8,128)S(1)}, f32[3,16,32,128]{3,2,1,0:T(8,128)}, u32[]{:S(2)}) copy-start(f32[3,16,32,128]{3,2,1,0:T(8,128)} %param.11) | copy-start | bytes 2359300
  1.6 6.6 %copy-start.1 = (f32[16,32,128]{2,1,0:T(8,128)S(1)}, f32[16,32,128]{2,1,0:T(8,128)}, u32[]{:S(2)}) copy-start(f32[16,32,128]{2,1,0:T(8,128)} %param.12) | copy-start | bytes 786436
  3.3 11.4 %copy-start.4 = (s32[1,1,2,16]{3,2,1,0:T(2,128)S(1)}, s32[1,1,2,16]{3,2,1,0:T(2,128)}, u32[]{:S(2)}) copy-start(s32[1,1,2,16]{3,2,1,0:T(2,128)} %param.15) | copy-start | bytes 388
  4.0 10.8 %copy-start.3 = (s32[1,1,2,16]{3,2,1,0:T(2,128)S(1)}, s32[1,1,2,16]{3,2,1,0:T(2,128)}, u32[]{:S(2)}) copy-start(s32[1,1,2,16]{3,2,1,0:T(2,128)} %param.16) | copy-start | bytes 388
  4.1 11.0 %copy-start.5 = (s32[1,1,2,16]{3,2,1,0:T(2,128)S(1)}, s32[1,1,2,16]{3,2,1,0:T(2,128)}, u32[]{:S(2)}) copy-start(s32[1,1,2,16]{3,2,1,0:T(2,128)} %param.14) | copy-start | bytes 388
  4.1 11.1 %copy-start.2 = (f32[4,128,128]{2,1,0:T(8,128)S(1)}, f32[4,128,128]{2,1,0:T(8,128)}, u32[]{:S(2)}) copy-start(f32[4,128,128]{2,1,0:T(8,128)} %param.13) | copy-start | bytes 786436
  4.9 10.4 %all-to-all-start = ((f32[3,2,16,128]{3,2,0,1:T(8,128)}), f32[3,2,16,128]{3,2,0,1:T(8,128)S(1)}, u32[]{:S(2)}, u32[]{:S(2)}) async-start(f32[3,2,16,128]{3,2,0,1:T(8,128)} %copy.57), calls=%async_computation | async-start | bytes 98304 | tf_op jit(solution)/shard_map/all_to_all | solution.py:77
  8.2 9.3 %collective-permute-start.4 = (f32[4,1,32,128]{3,2,1,0:T(8,128)S(1)}, f32[4,1,32,128]{3,2,1,0:T(8,128)S(1)}, u32[]{:S(2)}, u32[]{:S(2)}) collective-permute-start(f32[4,1,32,128]{3,2,1,0:T(8,128)S(1)} %get-tuple-element.10), channel_id=1, source_target_pairs={{0,2},{2,4},{4,6},{6,8},{8,10},{10,12},{12,14},{14,16},{16,18},{18... | collective-permute-start | bytes 196616 | tf_op jit(solution)/shard_map/ppermute | solution.py:20
  10.1 7.3 %collective-permute-start.5 = (f32[4,1,32,128]{3,2,1,0:T(8,128)S(1)}, f32[4,1,32,128]{3,2,1,0:T(8,128)S(1)}, u32[]{:S(2)}, u32[]{:S(2)}) collective-permute-start(f32[4,1,32,128]{3,2,1,0:T(8,128)S(1)} %get-tuple-element.11), channel_id=1, source_target_pairs={{2,0},{4,2},{6,4},{8,6},{10,8},{12,10},{14,12},{16,14},{18,16},{20... | collective-permute-start | bytes 196616 | tf_op jit(solution)/shard_map/ppermute | solution.py:22
  17.5 11.7 %collective-permute-start.6 = (f32[4,18,1,128]{3,2,1,0:T(1,128)S(1)}, f32[4,18,1,128]{3,2,1,0:T(1,128)S(1)}, u32[]{:S(2)}, u32[]{:S(2)}) collective-permute-start(f32[4,18,1,128]{3,2,1,0:T(1,128)S(1)} %get-tuple-element.8), channel_id=1, source_target_pairs={{0,1},{2,3},{4,5},{6,7},{8,9},{10,11},{12,13},{14,15},{16,17},{18,... | collective-permute-start | bytes 110600 | tf_op jit(solution)/shard_map/ppermute | solution.py:20
  21.4 7.8 %collective-permute-start.7 = (f32[4,18,1,128]{3,2,1,0:T(1,128)S(1)}, f32[4,18,1,128]{3,2,1,0:T(1,128)S(1)}, u32[]{:S(2)}, u32[]{:S(2)}) collective-permute-start(f32[4,18,1,128]{3,2,1,0:T(1,128)S(1)} %get-tuple-element.9), channel_id=1, source_target_pairs={{1,0},{3,2},{5,4},{7,6},{9,8},{11,10},{13,12},{15,14},{17,16},{19,... | collective-permute-start | bytes 110600 | tf_op jit(solution)/shard_map/ppermute | solution.py:22
  22.8 6.8 %collective-permute-start = (f32[3,2,32,128]{3,2,1,0:T(8,128)S(1)}, f32[3,2,32,128]{3,2,1,0:T(8,128)S(1)}, u32[]{:S(2)}, u32[]{:S(2)}) collective-permute-start(f32[3,2,32,128]{3,2,1,0:T(8,128)S(1)} %get-tuple-element.15), channel_id=1, source_target_pairs={{0,2},{2,4},{4,6},{6,8},{8,10},{10,12},{12,14},{14,16},{16,18},{18... | collective-permute-start | bytes 294920 | tf_op jit(solution)/shard_map/ppermute | solution.py:20
  24.7 6.7 %collective-permute-start.1 = (f32[3,2,32,128]{3,2,1,0:T(8,128)S(1)}, f32[3,2,32,128]{3,2,1,0:T(8,128)S(1)}, u32[]{:S(2)}, u32[]{:S(2)}) collective-permute-start(f32[3,2,32,128]{3,2,1,0:T(8,128)S(1)} %get-tuple-element.14), channel_id=1, source_target_pairs={{2,0},{4,2},{6,4},{8,6},{10,8},{12,10},{14,12},{16,14},{18,16},{20... | collective-permute-start | bytes 294920 | tf_op jit(solution)/shard_map/ppermute | solution.py:22
  31.5 6.4 %collective-permute-start.2 = (f32[3,20,2,128]{3,2,1,0:T(2,128)S(1)}, f32[3,20,2,128]{3,2,1,0:T(2,128)S(1)}, u32[]{:S(2)}, u32[]{:S(2)}) collective-permute-start(f32[3,20,2,128]{3,2,1,0:T(2,128)S(1)} %get-tuple-element.12), channel_id=1, source_target_pairs={{0,1},{2,3},{4,5},{6,7},{8,9},{10,11},{12,13},{14,15},{16,17},{18,... | collective-permute-start | bytes 184328 | tf_op jit(solution)/shard_map/ppermute | solution.py:20
  36.0 6.1 %collective-permute-start.3 = (f32[3,20,2,128]{3,2,1,0:T(2,128)S(1)}, f32[3,20,2,128]{3,2,1,0:T(2,128)S(1)}, u32[]{:S(2)}, u32[]{:S(2)}) collective-permute-start(f32[3,20,2,128]{3,2,1,0:T(2,128)S(1)} %get-tuple-element.13), channel_id=1, source_target_pairs={{1,0},{3,2},{5,4},{7,6},{9,8},{11,10},{13,12},{15,14},{17,16},{19,... | collective-permute-start | bytes 184328 | tf_op jit(solution)/shard_map/ppermute | solution.py:22
  46.6 7.3 %all-to-all-start.1 = ((f32[3,2,16,128]{3,2,0,1:T(8,128)}), f32[3,2,16,128]{3,2,0,1:T(8,128)S(1)}, u32[]{:S(2)}, u32[]{:S(2)}) async-start(f32[3,2,16,128]{3,2,0,1:T(8,128)} %copy.67), calls=%async_computation.1 | async-start | bytes 98304 | tf_op jit(solution)/shard_map/all_to_all | solution.py:123
where the time goes:
time: 57.3 us; the launch traced here: 56.8 us
  starting transfers between devices  30.5 us (53%)
  waiting for transfers between devices  10.6 us (18%)
  local copies, waits for them, and re-layouts  7.3 us (13%)
  other arithmetic  7.21 us (13%)
  matrix products  0.78 us (1%)
    ppermute x4, starting transfers between devices, extended(): lax.ppermute(tail, axis, [(i, (i + 1) % count) for i in range(ends)])  12.3 us
    ppermute x4, starting transfers between devices, extended(): lax.ppermute(head, axis, [((i + 1) % count, i) for i in range(ends)])  11.7 us
    ppermute x4, waiting for transfers between devices, extended(): lax.ppermute(head, axis, [((i + 1) % count, i) for i in range(ends)])  5.99 us
    all_to_all x1, waiting for transfers between devices, local(): lax.all_to_all(restricted, 'group', split_axis=1, concat_axis=1, tiled=True)  4.01 us
    all_to_all x1, starting transfers between devices, local(): lax.all_to_all(picked, 'group', split_axis=1, concat_axis=1, tiled=True)  3.28 us
    all_to_all x1, starting transfers between devices, local(): lax.all_to_all(restricted, 'group', split_axis=1, concat_axis=1, tiled=True)  3.28 us
    unnamed x18, local copies, waits for them, and re-layouts  2.04 us
    scatter-add x1, other arithmetic, local(): blocks.at[:, child_index].add(hanging)  1.64 us
  transfers between devices with their start and end apart: 10, of which 5 were waited for; matrix products, arithmetic and copies ran while one was open for 5% of the time, Pallas kernels for 0%

commit v1 on v0

v1 whole, which is shorter than its diff:
```python
import functools

import jax
import jax.numpy as jnp
from jax import lax
from jax.experimental import pallas as pl
from jax.experimental.pallas import tpu as pltpu
from jax.sharding import PartitionSpec as P

OMEGA = 2.0 / 3.0
KEEP = 1.0 / 3.0
MESH = pl.DeviceIdType.MESH
NT = (((1,), (1,)), ((), ()))


def split(value):
    high = value.astype(jnp.bfloat16)
    low = (value - high.astype(jnp.float32)).astype(jnp.bfloat16)
    return high, low


def column(row, size):
    first = lax.broadcasted_iota(jnp.int32, (size, size), 0)
    second = lax.broadcasted_iota(jnp.int32, (size, size), 1)
    spread = jnp.where(first == second, jnp.broadcast_to(row.astype(jnp.float32), (size, size)), 0.0)
    return jnp.sum(spread, axis=1, keepdims=True)


def lane_row(columns, slots):
    groups = len(columns)
    width = 2 * groups * slots
    first = lax.broadcasted_iota(jnp.int32, (slots, width), 0)
    second = lax.broadcasted_iota(jnp.int32, (slots, width), 1)
    total = jnp.zeros((slots, width), jnp.float32)
    for half in range(2):
        for group, col in enumerate(columns):
            base = (half * groups + group) * slots
            total = total + jnp.where(second - base == first, jnp.broadcast_to(col, (slots, width)), 0.0)
    return jnp.sum(total, axis=0, keepdims=True).astype(jnp.int32)


def kernel(
    curve_size, groups, rows_x, rows_y, nodes, slots, kinds, comps,
    field, source, mass, interp, parent_s, child_s, counts_s, parent_v, child_v, kind_v,
    out,
    con, mid, fin, src, wts, rhs, tab, pick, arr, base_rows, now_rows, res, back,
    x_in, y_out, y_in, s_out, s_in, k_out, k_in, y_mid, ext,
    load_sem, out_sem, send_sem, recv_sem, pick_send, pick_recv, back_send, back_recv,
):
    f32 = jnp.float32
    blocks = rows_x * rows_y
    mem = comps * slots
    c = lax.axis_index("curve")
    g = lax.axis_index("group")
    has_x = (c > 0, c < curve_size - 1)
    has_y = (g > 0, g < groups - 1)
    step = (-1, 1)

    loads = [
        pltpu.make_async_copy(field, con.at[:, pl.ds(rows_y, blocks), :], load_sem.at[0]),
        pltpu.make_async_copy(mass, wts.at[pl.ds(rows_y, blocks), :], load_sem.at[1]),
        pltpu.make_async_copy(source, src.at[:, pl.ds(rows_y, blocks), :], load_sem.at[2]),
        pltpu.make_async_copy(interp, tab, load_sem.at[3]),
    ]
    for load in loads:
        load.start()

    barrier = pltpu.get_barrier_semaphore()
    for o in range(1, groups):
        pl.semaphore_signal(barrier, inc=1, device_id=(c, lax.rem(g + o, groups)), device_id_type=MESH)
    for a in range(2):
        @pl.when(has_x[a])
        def _():
            pl.semaphore_signal(barrier, inc=1, device_id=(c + step[a], g), device_id_type=MESH)
        for b in range(2):
            @pl.when(jnp.logical_and(has_x[a], has_y[b]))
            def _():
                pl.semaphore_signal(barrier, inc=1, device_id=(c + step[a], g + step[b]), device_id_type=MESH)
    one = lambda flag: jnp.where(flag, 1, 0)
    wide = one(has_x[0]) + one(has_x[1])
    tall = one(has_y[0]) + one(has_y[1])
    pl.semaphore_wait(barrier, groups - 1 + wide + wide * tall)

    def remote(src_ref, dst_ref, sent, landed, device):
        return pltpu.make_async_remote_copy(
            src_ref=src_ref, dst_ref=dst_ref, send_sem=send_sem.at[sent], recv_sem=recv_sem.at[landed],
            device_id=device, device_id_type=MESH,
        )

    def source_x(a, arriving=False):
        side = a if arriving else 1 - a
        edge = 0 if a == 0 else blocks - rows_y
        land = 0 if side == 0 else blocks + rows_y
        there = (c + step[a], g)
        return (
            remote(source.at[:, pl.ds(edge, rows_y), :], src.at[:, pl.ds(land, rows_y), :], a, side, there),
            remote(mass.at[pl.ds(edge, rows_y), :], wts.at[pl.ds(land, rows_y), :], 2 + a, 2 + side, there),
        )

    def source_y(b, arriving=False):
        side = b if arriving else 1 - b
        return remote(s_out.at[b], s_in.at[side], 4 + b, 4 + side, (c, g + step[b]))

    def halo_x(a, arriving=False):
        side = a if arriving else 1 - a
        edge = rows_y if a == 0 else blocks - rows_y
        return remote(con.at[:, pl.ds(edge, 2 * rows_y), :], x_in.at[side], 6 + a, 6 + side, (c + step[a], g))

    def halo_y(b, arriving=False):
        side = b if arriving else 1 - b
        return remote(y_out.at[b], y_in.at[side], 8 + b, 8 + side, (c, g + step[b]))

    def corner(a, b, arriving=False):
        side = 2 * a + b if arriving else 2 * (1 - a) + (1 - b)
        return remote(k_out.at[2 * a + b], k_in.at[side], 10 + 2 * a + b, 10 + side, (c + step[a], g + step[b]))

    def picks(o):
        d = lax.rem(g + o, groups)
        return pltpu.make_async_remote_copy(
            src_ref=pick.at[o], dst_ref=arr.at[g], send_sem=pick_send.at[o], recv_sem=pick_recv.at[o],
            device_id=(c, d), device_id_type=MESH,
        )

    def returns(o):
        d = lax.rem(g + o, groups)
        return pltpu.make_async_remote_copy(
            src_ref=res.at[d], dst_ref=back.at[g], send_sem=back_send.at[o], recv_sem=back_recv.at[o],
            device_id=(c, d), device_id_type=MESH,
        )

    loads[0].wait()
    slot_of = lax.broadcasted_iota(jnp.int32, (slots, nodes), 0)
    for o in list(range(1, groups)) + [0]:
        d = lax.rem(g + o, groups)
        for k in range(slots):
            p = parent_s[0, 0, d, k]
            for m in range(comps):
                pick[o, pl.ds(m * slots + k, 1), :] = con[m, pl.ds(rows_y + p, 1), :]
        live = slot_of < counts_s[0, 0, d]
        for m in range(comps):
            part = pl.ds(m * slots, slots)
            pick[o, part, :] = jnp.where(live, pick[o, part, :], 0.0)
        if o:
            picks(o).start()
    arr[g] = pick[0]

    for a in range(2):
        @pl.when(has_x[a])
        def _():
            for copy in source_x(a):
                copy.start()

    loads[1].wait()
    loads[2].wait()
    for b in range(2):
        row = 0 if b == 0 else rows_y - 1
        for m in range(comps):
            s_out[b, pl.ds(m * rows_x, rows_x), :] = src[m, pl.ds(rows_y + row, rows_x, stride=rows_y), :]
        s_out[b, pl.ds(comps * rows_x, rows_x), :] = wts[pl.ds(rows_y + row, rows_x, stride=rows_y), :]

        @pl.when(has_y[b])
        def _():
            source_y(b).start()

    span = 2 * rows_y if rows_x % 2 == 0 else rows_y
    spans = blocks // span
    for t in range(spans):
        rows = pl.ds(rows_y + t * span, span)
        w = OMEGA / (6.0 + wts[rows, :])
        ext[pl.ds(rows_y + t * span, span), :] = w
        for m in range(comps):
            rhs[m, rows, :] = w * src[m, rows, :]
    zero_plane = jnp.zeros((rows_y, nodes), f32)
    for m in range(comps):
        con[m, pl.ds(0, rows_y), :] = zero_plane
        con[m, pl.ds(blocks + rows_y, rows_y), :] = zero_plane
    loads[3].wait()
    tab_high, tab_low = split(tab[...])
    kind_now = kind_v[0, 0]
    child_now = child_v[0, 0]
    parent_now = parent_v[0, 0]
    kind_of = []
    for s in range(groups):
        kind_col = jnp.broadcast_to(column(kind_now[s:s + 1, :], slots), (slots, nodes))
        kind_of += [kind_col] * comps
    kind_of = jnp.concatenate(kind_of, axis=0)
    child_row = lane_row([column(child_now[s:s + 1, :], slots) for s in range(groups)], slots)
    live_cols = []
    for s in range(groups):
        col = column(parent_now[s:s + 1, :], slots)
        ahead = lax.broadcasted_iota(jnp.int32, (slots, 1), 0) < counts_s[0, 0, s]
        live_cols.append(jnp.where(ahead, col, -1.0))
    parent_row = lane_row(live_cols, slots)

    def table_of(values):
        pieces = []
        for s in range(groups):
            pieces.append(jnp.concatenate(
                [values[(s * comps + m) * slots:(s * comps + m + 1) * slots, :] for m in range(comps)], axis=1))
        high, low = split(jnp.concatenate(pieces, axis=0))
        return jnp.concatenate([high, low], axis=0)

    piece = 4 * rows_y if rows_x % 4 == 0 else rows_y
    pieces = blocks // piece

    def spread(index_row, table, t):
        place = lax.broadcasted_iota(jnp.int32, (piece, 2 * groups * slots), 0) + t * piece
        hot = jnp.where(place == index_row, 1.0, 0.0).astype(jnp.bfloat16)
        return jnp.dot(hot, table, preferred_element_type=f32)

    for o in range(1, groups):
        picks(o).wait_recv()
    flat = arr[...].reshape(groups * mem, nodes)
    wide_rows = jnp.concatenate([jnp.where(kind_of == float(k), flat, 0.0) for k in range(kinds)], axis=1)
    high, low = split(wide_rows)
    hang = (
        jnp.dot(high, tab_high, preferred_element_type=f32)
        + jnp.dot(high, tab_low, preferred_element_type=f32)
        + jnp.dot(low, tab_high, preferred_element_type=f32)
    )
    table = table_of(hang)
    order = [0, pieces - 1] + list(range(1, pieces - 1))
    for at, t in enumerate(order):
        added = spread(child_row, table, t)
        for m in range(comps):
            rows = pl.ds(rows_y + t * piece, piece)
            con[m, rows, :] = con[m, rows, :] + added[:, m * nodes:(m + 1) * nodes]
        if at == 1:
            for a in range(2):
                @pl.when(has_x[a])
                def _():
                    halo_x(a).start()
            for a in range(2):
                for b in range(2):
                    x = 0 if a == 0 else rows_x - 1
                    y = 0 if b == 0 else rows_y - 1
                    for m in range(comps):
                        k_out[2 * a + b, pl.ds(m, 1), :] = con[m, pl.ds(rows_y + x * rows_y + y, 1), :]

                    @pl.when(jnp.logical_and(has_x[a], has_y[b]))
                    def _():
                        corner(a, b).start()
    for b in range(2):
        for j in range(2):
            row = j if b == 0 else rows_y - 1 - j
            for m in range(comps):
                y_out[b, pl.ds((j * comps + m) * rows_x, rows_x), :] = con[m, pl.ds(rows_y + row, rows_x, stride=rows_y), :]

        @pl.when(has_y[b])
        def _():
            halo_y(b).start()

    lane = lax.broadcasted_iota(jnp.int32, (1, nodes), 1)

    def along_z(v):
        up = jnp.where(lane == 0, 0.0, pltpu.roll(v, 1, 1))
        down = jnp.where(lane == nodes - 1, 0.0, pltpu.roll(v, nodes - 1, 1))
        return up + down

    sub = lax.broadcasted_iota(jnp.int32, (span, nodes), 0)
    is_first = sub == 0
    is_last = sub == rows_y - 1
    for t in range(1, span // rows_y):
        is_first = jnp.logical_or(is_first, sub == t * rows_y)
        is_last = jnp.logical_or(is_last, sub == (t + 1) * rows_y - 1)

    def core(state, m, t):
        at = rows_y + t * span
        centre = state[m, pl.ds(at, span), :]
        beside = state[m, pl.ds(at - rows_y, span), :] + state[m, pl.ds(at + rows_y, span), :]
        beside = beside + jnp.where(is_first, 0.0, state[m, pl.ds(at - 1, span), :])
        beside = beside + jnp.where(is_last, 0.0, state[m, pl.ds(at + 1, span), :])
        beside = beside + along_z(centre)
        return KEEP * centre + ext[pl.ds(at, span), :] * beside + rhs[m, pl.ds(at, span), :]

    for t in range(spans):
        for m in range(comps):
            mid[m, pl.ds(rows_y + t * span, span), :] = core(con, m, t)

    for s in range(groups):
        for k in range(slots):
            q = child_s[0, 0, s, k]
            for m in range(comps):
                base_rows[pl.ds((s * comps + m) * slots + k, 1), :] = con[m, pl.ds(rows_y + q, 1), :]

    for a in range(2):
        for b in range(2):
            both = jnp.logical_and(has_x[a], has_y[b])

            @pl.when(both)
            def _():
                corner(a, b, True).wait_recv()

            @pl.when(jnp.logical_not(both))
            def _():
                k_in[2 * a + b] = jnp.zeros((8, nodes), f32)
    top = lax.broadcasted_iota(jnp.int32, (rows_y, nodes), 0)
    for a in range(2):
        inside = rows_y if a == 0 else blocks
        plane = 0 if a == 0 else blocks + rows_y
        near = rows_y if a == 0 else 0
        far = 0 if a == 0 else rows_y

        @pl.when(has_x[a])
        def _():
            for copy in source_x(a, True):
                copy.wait_recv()
            halo_x(a, True).wait_recv()
            w_in = ext[pl.ds(inside, rows_y), :]
            w = OMEGA / (6.0 + wts[pl.ds(plane, rows_y), :])
            for m in range(comps):
                own = x_in[a, m, pl.ds(near, rows_y), :]
                mid[m, pl.ds(inside, rows_y), :] = mid[m, pl.ds(inside, rows_y), :] + w_in * own
                beside = x_in[a, m, pl.ds(far, rows_y), :] + con[m, pl.ds(inside, rows_y), :]
                low_end = jnp.broadcast_to(k_in[2 * a, pl.ds(m, 1), :], (rows_y, nodes))
                high_end = jnp.broadcast_to(k_in[2 * a + 1, pl.ds(m, 1), :], (rows_y, nodes))
                beside = beside + jnp.where(top == 0, low_end, pltpu.roll(own, 1, 0))
                beside = beside + jnp.where(top == rows_y - 1, high_end, pltpu.roll(own, rows_y - 1, 0))
                beside = beside + along_z(own) + src[m, pl.ds(plane, rows_y), :]
                mid[m, pl.ds(plane, rows_y), :] = KEEP * own + w * beside

        @pl.when(jnp.logical_not(has_x[a]))
        def _():
            for m in range(comps):
                mid[m, pl.ds(plane, rows_y), :] = zero_plane

    left = lax.broadcasted_iota(jnp.int32, (rows_x, nodes), 0)
    for b in range(2):
        row = 0 if b == 0 else rows_y - 1
        edge = pl.ds(rows_y + row, rows_x, stride=rows_y)

        @pl.when(has_y[b])
        def _():
            source_y(b, True).wait_recv()
            halo_y(b, True).wait_recv()
            w_in = ext[edge, :]
            w = OMEGA / (6.0 + s_in[b, pl.ds(comps * rows_x, rows_x), :])
            for m in range(comps):
                own = y_in[b, pl.ds(m * rows_x, rows_x), :]
                mid[m, edge, :] = mid[m, edge, :] + w_in * own
                beside = y_in[b, pl.ds((comps + m) * rows_x, rows_x), :] + con[m, edge, :]
                low_end = jnp.broadcast_to(k_in[b, pl.ds(m, 1), :], (rows_x, nodes))
                high_end = jnp.broadcast_to(k_in[2 + b, pl.ds(m, 1), :], (rows_x, nodes))
                beside = beside + jnp.where(left == 0, low_end, pltpu.roll(own, 1, 0))
                beside = beside + jnp.where(left == rows_x - 1, high_end, pltpu.roll(own, rows_x - 1, 0))
                beside = beside + along_z(own) + s_in[b, pl.ds(m * rows_x, rows_x), :]
                y_mid[b, pl.ds(m * rows_x, rows_x), :] = KEEP * own + w * beside

    for t in range(spans):
        for m in range(comps):
            fin[m, pl.ds(t * span, span), :] = core(mid, m, t)
    for b in range(2):
        row = 0 if b == 0 else rows_y - 1

        @pl.when(has_y[b])
        def _():
            w_in = ext[pl.ds(rows_y + row, rows_x, stride=rows_y), :]
            edge = pl.ds(row, rows_x, stride=rows_y)
            for m in range(comps):
                fin[m, edge, :] = fin[m, edge, :] + w_in * y_mid[b, pl.ds(m * rows_x, rows_x), :]

    for s in range(groups):
        for k in range(slots):
            q = child_s[0, 0, s, k]
            for m in range(comps):
                now_rows[pl.ds((s * comps + m) * slots + k, 1), :] = fin[m, pl.ds(q, 1), :]
    high, low = split(now_rows[...] - base_rows[...])
    product = (
        lax.dot_general(high, tab_high, NT, preferred_element_type=f32)
        + lax.dot_general(high, tab_low, NT, preferred_element_type=f32)
        + lax.dot_general(low, tab_high, NT, preferred_element_type=f32)
    )
    chosen = jnp.zeros((groups * mem, nodes), f32)
    for k in range(kinds):
        chosen = chosen + jnp.where(kind_of == float(k), product[:, k * nodes:(k + 1) * nodes], 0.0)
    res[...] = chosen.reshape(groups, mem, nodes)
    for o in range(1, groups):
        returns(o).start()
    back[g] = res[g]
    for o in range(1, groups):
        returns(o).wait_recv()
    table = table_of(back[...].reshape(groups * mem, nodes))
    stores = []
    for t in range(pieces):
        added = spread(parent_row, table, t)
        rows = pl.ds(t * piece, piece)
        for m in range(comps):
            fin[m, rows, :] = fin[m, rows, :] + added[:, m * nodes:(m + 1) * nodes]
        store = pltpu.make_async_copy(fin.at[:, rows, :], out.at[:, rows, :], out_sem.at[t])
        store.start()
        stores.append(store)

    for o in range(1, groups):
        picks(o).wait_send()
        returns(o).wait_send()
    for a in range(2):
        @pl.when(has_x[a])
        def _():
            for copy in source_x(a):
                copy.wait_send()
            halo_x(a).wait_send()

        @pl.when(has_y[a])
        def _():
            source_y(a).wait_send()
            halo_y(a).wait_send()
        for b in range(2):
            @pl.when(jnp.logical_and(has_x[a], has_y[b]))
            def _():
                corner(a, b).wait_send()
    for store in stores:
        store.wait()


def local(curve_size, groups, field, source, mass, interp, parent_list, child_list, child_kind, counts):
    comps, rows_x, rows_y, nodes = field.shape
    slots = parent_list.shape[3]
    kinds = interp.shape[0]
    blocks = rows_x * rows_y
    deep = blocks + 2 * rows_y
    mem = comps * slots
    pieces = rows_x // 4 if rows_x % 4 == 0 else rows_x
    f32 = jnp.float32
    hbm = pl.BlockSpec(memory_space=pl.ANY)
    vmem = pl.BlockSpec(memory_space=pltpu.VMEM)
    smem = pl.BlockSpec(memory_space=pltpu.SMEM)
    dma = pltpu.SemaphoreType.DMA
    out = pl.pallas_call(
        functools.partial(kernel, curve_size, groups, rows_x, rows_y, nodes, slots, kinds, comps),
        out_shape=jax.ShapeDtypeStruct((comps, blocks, nodes), f32),
        in_specs=[hbm] * 4 + [smem] * 3 + [vmem] * 3,
        out_specs=hbm,
        scratch_shapes=[
            pltpu.VMEM((comps, deep, nodes), f32),
            pltpu.VMEM((comps, deep, nodes), f32),
            pltpu.VMEM((comps, blocks, nodes), f32),
            pltpu.VMEM((comps, deep, nodes), f32),
            pltpu.VMEM((deep, nodes), f32),
            pltpu.VMEM((comps, deep, nodes), f32),
            pltpu.VMEM((kinds * nodes, nodes), f32),
            pltpu.VMEM((groups, mem, nodes), f32),
            pltpu.VMEM((groups, mem, nodes), f32),
            pltpu.VMEM((groups * mem, nodes), f32),
            pltpu.VMEM((groups * mem, nodes), f32),
            pltpu.VMEM((groups, mem, nodes), f32),
            pltpu.VMEM((groups, mem, nodes), f32),
            pltpu.VMEM((2, comps, 2 * rows_y, nodes), f32),
            pltpu.VMEM((2, 2 * comps * rows_x, nodes), f32),
            pltpu.VMEM((2, 2 * comps * rows_x, nodes), f32),
            pltpu.VMEM((2, (comps + 1) * rows_x, nodes), f32),
            pltpu.VMEM((2, (comps + 1) * rows_x, nodes), f32),
            pltpu.VMEM((4, 8, nodes), f32),
            pltpu.VMEM((4, 8, nodes), f32),
            pltpu.VMEM((2, comps * rows_x, nodes), f32),
            pltpu.VMEM((deep, nodes), f32),
            dma((4,)),
            dma((pieces,)),
            dma((14,)),
            dma((14,)),
            dma((groups,)),
            dma((groups,)),
            dma((groups,)),
            dma((groups,)),
        ],
        compiler_params=pltpu.CompilerParams(
            collective_id=0, has_side_effects=True, vmem_limit_bytes=24 * 1024 * 1024
        ),
    )(
        field.reshape(comps, blocks, nodes),
        source.reshape(comps, blocks, nodes),
        mass.reshape(blocks, nodes),
        interp.reshape(kinds * nodes, nodes),
        parent_list, child_list, counts, parent_list, child_list, child_kind,
    )
    return out.reshape(comps, rows_x, rows_y, nodes)


def solution(mesh):
    in_specs = (
        P(None, "curve", "group", None),
        P(None, "curve", "group", None),
        P("curve", "group", None),
        P(),
        P("curve", "group", None, None),
        P("curve", "group", None, None),
        P("curve", "group", None, None),
        P("curve", "group", None),
    )
    out_specs = P(None, "curve", "group", None)
    body = functools.partial(local, mesh.shape["curve"], mesh.shape["group"])
    return jax.shard_map(body, mesh=mesh, in_specs=in_specs, out_specs=out_specs, check_vma=False)
```

time: 57.3 us -> 21.6 us (0.38)
  the two profiles are of different devices: /device:TPU:8 before, /device:TPU:9 now
where the time goes in v1:
time: 21.6 us; the launch traced here: 21.4 us
  Pallas kernels  15.6 us (72%)
  local copies, waits for them, and re-layouts  5.75 us (27%)
    pallas_call x1, Pallas kernels, local(): pl.pallas_call(functools.partial(kernel, curve_size, groups, rows_x, rows...  15.6 us
    unnamed x17, local copies, waits for them, and re-layouts  5.75 us

profile of v1, /device:TPU:9, one launch (start us, length us, event | category | flops | bytes accessed | tf_op | source)
XLA Modules:
  0.0 21.4 jit_solution(1616166261169502899)
XLA Ops:
  0.0 0.0 copy-start.5
  0.0 0.0 copy-start.6
  0.0 0.0 copy-start.4
  0.0 0.0 copy-start.7
  0.0 0.7 %copy-done.5 = s32[1,1,2,16]{3,2,1,0:T(2,128)S(1)} copy-done((s32[1,1,2,16]{3,2,1,0:T(2,128)S(1)}, s32[1,1,2,16]{3,2,1,0:T(2,128)}, u32[]{:S(2)}) %copy-start.5) | copy-done | bytes 152
  0.7 0.0 copy-done.6
  0.7 0.0 copy-done.4
  0.7 0.0 copy-done.7
  0.7 0.0 copy-start
  0.7 1.1 %copy-done = f32[3,16,32,128]{3,2,1,0:T(8,128)S(1)} copy-done((f32[3,16,32,128]{3,2,1,0:T(8,128)S(1)}, f32[3,16,32,128]{3,2,1,0:T(8,128)}, u32[]{:S(2)}) %copy-start) | copy-done | bytes 786456
  1.8 0.0 copy-start.1
  1.9 1.1 %copy-done.1 = f32[3,16,32,128]{3,2,1,0:T(8,128)S(1)} copy-done((f32[3,16,32,128]{3,2,1,0:T(8,128)S(1)}, f32[3,16,32,128]{3,2,1,0:T(8,128)}, u32[]{:S(2)}) %copy-start.1) | copy-done | bytes 786456
  3.0 0.0 copy-start.2
  3.0 0.9 %copy-done.2 = f32[16,32,128]{2,1,0:T(8,128)S(1)} copy-done((f32[16,32,128]{2,1,0:T(8,128)S(1)}, f32[16,32,128]{2,1,0:T(8,128)}, u32[]{:S(2)}) %copy-start.2) | copy-done | bytes 262168
  3.9 0.0 copy-start.3
  3.9 0.9 %copy-done.3 = f32[4,128,128]{2,1,0:T(8,128)S(1)} copy-done((f32[4,128,128]{2,1,0:T(8,128)S(1)}, f32[4,128,128]{2,1,0:T(8,128)}, u32[]{:S(2)}) %copy-start.3) | copy-done | bytes 262168
  4.9 15.6 %shard_map.82 = f32[3,512,128]{2,1,0:T(8,128)S(1)} custom-call(f32[3,512,128]{2,1,0:T(8,128)S(1)} %bitcast.6, f32[3,512,128]{2,1,0:T(8,128)S(1)} %bitcast.7, f32[512,128]{1,0:T(8,128)S(1)} %bitcast.8, f32[512,128]{1,0:T(8,128)S(1)} %bitcast.9, s32[1,1,2,16]{3,2,1,0:T(2,128)S(1)} %copy-done.4, s32[1,1,2,16]{3,2,1,0:T(2,128)S(1)} %copy-done.5, ...), custom_call_target="tpu_custom_call" | custom-call | tf_op jit(solution)/shard_map/pallas_call | solution.py:428
  20.5 0.9 %copy.10 = f32[3,16,32,128]{3,2,1,0:T(8,128)} copy(f32[3,16,32,128]{3,2,1,0:T(8,128)S(1)} %bitcast.5) | data formatting | bytes 1572864
Async XLA Ops:
  0.0 0.7 %copy-start.5 = (s32[1,1,2,16]{3,2,1,0:T(2,128)S(1)}, s32[1,1,2,16]{3,2,1,0:T(2,128)}, u32[]{:S(2)}) copy-start(s32[1,1,2,16]{3,2,1,0:T(2,128)} %child_v.1) | copy-start | bytes 388
  0.0 0.7 %copy-start.6 = (s32[1,1,2,16]{3,2,1,0:T(2,128)S(1)}, s32[1,1,2,16]{3,2,1,0:T(2,128)}, u32[]{:S(2)}) copy-start(s32[1,1,2,16]{3,2,1,0:T(2,128)} %kind_v.1) | copy-start | bytes 388
  0.0 0.7 %copy-start.4 = (s32[1,1,2,16]{3,2,1,0:T(2,128)S(1)}, s32[1,1,2,16]{3,2,1,0:T(2,128)}, u32[]{:S(2)}) copy-start(s32[1,1,2,16]{3,2,1,0:T(2,128)} %parent_v.1) | copy-start | bytes 388
  0.0 0.7 %copy-start.7 = (s32[1,1,2]{2,1,0:T(1,128)S(1)}, s32[1,1,2]{2,1,0:T(1,128)}, u32[]{:S(2)}) copy-start(s32[1,1,2]{2,1,0:T(1,128)} %counts_s.1) | copy-start | bytes 28
  0.7 1.1 %copy-start = (f32[3,16,32,128]{3,2,1,0:T(8,128)S(1)}, f32[3,16,32,128]{3,2,1,0:T(8,128)}, u32[]{:S(2)}) copy-start(f32[3,16,32,128]{3,2,1,0:T(8,128)} %param.8) | copy-start | bytes 2359300
  1.8 1.1 %copy-start.1 = (f32[3,16,32,128]{3,2,1,0:T(8,128)S(1)}, f32[3,16,32,128]{3,2,1,0:T(8,128)}, u32[]{:S(2)}) copy-start(f32[3,16,32,128]{3,2,1,0:T(8,128)} %param.9) | copy-start | bytes 2359300
  3.0 0.9 %copy-start.2 = (f32[16,32,128]{2,1,0:T(8,128)S(1)}, f32[16,32,128]{2,1,0:T(8,128)}, u32[]{:S(2)}) copy-start(f32[16,32,128]{2,1,0:T(8,128)} %param.10) | copy-start | bytes 786436
  3.9 0.9 %copy-start.3 = (f32[4,128,128]{2,1,0:T(8,128)S(1)}, f32[4,128,128]{2,1,0:T(8,128)}, u32[]{:S(2)}) copy-start(f32[4,128,128]{2,1,0:T(8,128)} %param.11) | copy-start | bytes 786436

commit v2 on v1

--- a/solution.py
+++ b/solution.py
@@ -41,11 +41,12 @@
 
 def kernel(
     curve_size, groups, rows_x, rows_y, nodes, slots, kinds, comps,
-    field, source, mass, interp, parent_s, child_s, counts_s, parent_v, child_v, kind_v,
-    out,
-    con, mid, fin, src, wts, rhs, tab, pick, arr, base_rows, now_rows, res, back,
+    field, source, mass, interp, parent_list, child_list, child_kind, counts,
+    fin,
+    con, mid, src, wts, rhs, tab, pick, arr, base_rows, now_rows, res, back,
     x_in, y_out, y_in, s_out, s_in, k_out, k_in, y_mid, ext,
-    load_sem, out_sem, send_sem, recv_sem, pick_send, pick_recv, back_send, back_recv,
+    parent_s, child_s, counts_s, parent_v, child_v, kind_v,
+    load_sem, send_sem, recv_sem, pick_send, pick_recv, back_send, back_recv,
 ):
     f32 = jnp.float32
     blocks = rows_x * rows_y
@@ -56,13 +57,22 @@
     has_y = (g > 0, g < groups - 1)
     step = (-1, 1)
 
+    lists = [
+        pltpu.make_async_copy(parent_list, parent_s, load_sem.at[4]),
+        pltpu.make_async_copy(counts, counts_s, load_sem.at[5]),
+        pltpu.make_async_copy(child_list, child_s, load_sem.at[6]),
+        pltpu.make_async_copy(parent_list, parent_v, load_sem.at[7]),
+        pltpu.make_async_copy(child_list, child_v, load_sem.at[8]),
+        pltpu.make_async_copy(child_kind, kind_v, load_sem.at[9]),
+    ]
     loads = [
         pltpu.make_async_copy(field, con.at[:, pl.ds(rows_y, blocks), :], load_sem.at[0]),
         pltpu.make_async_copy(mass, wts.at[pl.ds(rows_y, blocks), :], load_sem.at[1]),
         pltpu.make_async_copy(source, src.at[:, pl.ds(rows_y, blocks), :], load_sem.at[2]),
         pltpu.make_async_copy(interp, tab, load_sem.at[3]),
     ]
-    for load in loads:
+    loads[0].start()
+    for load in lists + loads[1:]:
         load.start()
 
     barrier = pltpu.get_barrier_semaphore()
@@ -128,6 +138,8 @@
             device_id=(c, d), device_id_type=MESH,
         )
 
+    for load in lists:
+        load.wait()
     loads[0].wait()
     slot_of = lax.broadcasted_iota(jnp.int32, (slots, nodes), 0)
     for o in list(range(1, groups)) + [0]:
@@ -380,15 +392,11 @@
     for o in range(1, groups):
         returns(o).wait_recv()
     table = table_of(back[...].reshape(groups * mem, nodes))
-    stores = []
     for t in range(pieces):
         added = spread(parent_row, table, t)
         rows = pl.ds(t * piece, piece)
         for m in range(comps):
             fin[m, rows, :] = fin[m, rows, :] + added[:, m * nodes:(m + 1) * nodes]
-        store = pltpu.make_async_copy(fin.at[:, rows, :], out.at[:, rows, :], out_sem.at[t])
-        store.start()
-        stores.append(store)
 
     for o in range(1, groups):
         picks(o).wait_send()
@@ -408,8 +416,6 @@
             @pl.when(jnp.logical_and(has_x[a], has_y[b]))
             def _():
                 corner(a, b).wait_send()
-    for store in stores:
-        store.wait()
 
 
 def local(curve_size, groups, field, source, mass, interp, parent_list, child_list, child_kind, counts):
@@ -419,21 +425,18 @@
     blocks = rows_x * rows_y
     deep = blocks + 2 * rows_y
     mem = comps * slots
-    pieces = rows_x // 4 if rows_x % 4 == 0 else rows_x
     f32 = jnp.float32
-    hbm = pl.BlockSpec(memory_space=pl.ANY)
+    hbm = pl.BlockSpec(memory_space=pltpu.HBM)
     vmem = pl.BlockSpec(memory_space=pltpu.VMEM)
-    smem = pl.BlockSpec(memory_space=pltpu.SMEM)
     dma = pltpu.SemaphoreType.DMA
     out = pl.pallas_call(
         functools.partial(kernel, curve_size, groups, rows_x, rows_y, nodes, slots, kinds, comps),
         out_shape=jax.ShapeDtypeStruct((comps, blocks, nodes), f32),
-        in_specs=[hbm] * 4 + [smem] * 3 + [vmem] * 3,
-        out_specs=hbm,
+        in_specs=[hbm] * 8,
+        out_specs=vmem,
         scratch_shapes=[
             pltpu.VMEM((comps, deep, nodes), f32),
             pltpu.VMEM((comps, deep, nodes), f32),
-            pltpu.VMEM((comps, blocks, nodes), f32),
             pltpu.VMEM((comps, deep, nodes), f32),
             pltpu.VMEM((deep, nodes), f32),
             pltpu.VMEM((comps, deep, nodes), f32),
@@ -453,8 +456,13 @@
             pltpu.VMEM((4, 8, nodes), f32),
             pltpu.VMEM((2, comps * rows_x, nodes), f32),
             pltpu.VMEM((deep, nodes), f32),
-            dma((4,)),
-            dma((pieces,)),
+            pltpu.SMEM(parent_list.shape, jnp.int32),
+            pltpu.SMEM(child_list.shape, jnp.int32),
+            pltpu.SMEM(counts.shape, jnp.int32),
+            pltpu.VMEM(parent_list.shape, jnp.int32),
+            pltpu.VMEM(child_list.shape, jnp.int32),
+            pltpu.VMEM(child_kind.shape, jnp.int32),
+            dma((10,)),
             dma((14,)),
             dma((14,)),
             dma((groups,)),
@@ -463,14 +471,14 @@
             dma((groups,)),
         ],
         compiler_params=pltpu.CompilerParams(
-            collective_id=0, has_side_effects=True, vmem_limit_bytes=24 * 1024 * 1024
+            collective_id=0, has_side_effects=True, vmem_limit_bytes=60 * 1024 * 1024
         ),
     )(
         field.reshape(comps, blocks, nodes),
         source.reshape(comps, blocks, nodes),
         mass.reshape(blocks, nodes),
         interp.reshape(kinds * nodes, nodes),
-        parent_list, child_list, counts, parent_list, child_list, child_kind,
+        parent_list, child_list, child_kind, counts,
     )
     return out.reshape(comps, rows_x, rows_y, nodes)
 

time: 21.6 us -> 17.4 us (0.81)
  the two profiles are of different devices: /device:TPU:9 before, /device:TPU:0 now
where the time goes in v2:
time: 17.4 us; the launch traced here: 17.3 us
  Pallas kernels  15.2 us (87%)
  local copies, waits for them, and re-layouts  2.06 us (12%)
    pallas_call x1, Pallas kernels, local(): pl.pallas_call(functools.partial(kernel, curve_size, groups, rows_x, rows...  15.2 us
    unnamed x1, local copies, waits for them, and re-layouts  2.06 us

profile of v2, /device:TPU:0, one launch (start us, length us, event | category | flops | bytes accessed | tf_op | source)
XLA Modules:
  0.0 17.3 jit_solution(14658767970573706671)
XLA Ops:
  0.0 15.2 %shard_map.82 = f32[3,512,128]{2,1,0:T(8,128)} custom-call(f32[3,512,128]{2,1,0:T(8,128)} %bitcast.6, f32[3,512,128]{2,1,0:T(8,128)} %bitcast.7, f32[512,128]{1,0:T(8,128)} %bitcast.8, f32[512,128]{1,0:T(8,128)} %bitcast.9, s32[1,1,2,16]{3,2,1,0:T(2,128)} %parent_list.1, s32[1,1,2,16]{3,2,1,0:T(2,128)} %child_list.1, s32[1,1,2,16]{3,2,1,0:T(2,128)} %child_kind.1, ...), custom_call_target="tpu_custom_call" | custom-call | tf_op jit(solution)/shard_map/pallas_call | solution.py:432
  15.2 2.1 %copy.10 = f32[3,16,32,128]{3,2,1,0:T(8,128)} copy(f32[3,16,32,128]{3,2,1,0:T(8,128)} %bitcast.5) | data formatting | bytes 1572864

commit v3 on v2

--- a/solution.py
+++ b/solution.py
@@ -42,11 +42,11 @@
 def kernel(
     curve_size, groups, rows_x, rows_y, nodes, slots, kinds, comps,
     field, source, mass, interp, parent_list, child_list, child_kind, counts,
-    fin,
-    con, mid, src, wts, rhs, tab, pick, arr, base_rows, now_rows, res, back,
+    out,
+    con, mid, fin, src, wts, rhs, tab, pick, arr, base_rows, now_rows, res, back,
     x_in, y_out, y_in, s_out, s_in, k_out, k_in, y_mid, ext,
     parent_s, child_s, counts_s, parent_v, child_v, kind_v,
-    load_sem, send_sem, recv_sem, pick_send, pick_recv, back_send, back_recv,
+    load_sem, out_sem, send_sem, recv_sem, pick_send, pick_recv, back_send, back_recv,
 ):
     f32 = jnp.float32
     blocks = rows_x * rows_y
@@ -392,11 +392,15 @@
     for o in range(1, groups):
         returns(o).wait_recv()
     table = table_of(back[...].reshape(groups * mem, nodes))
+    stores = []
     for t in range(pieces):
         added = spread(parent_row, table, t)
         rows = pl.ds(t * piece, piece)
         for m in range(comps):
             fin[m, rows, :] = fin[m, rows, :] + added[:, m * nodes:(m + 1) * nodes]
+        store = pltpu.make_async_copy(fin.at[:, rows, :], out.at[:, rows, :], out_sem.at[t])
+        store.start()
+        stores.append(store)
 
     for o in range(1, groups):
         picks(o).wait_send()
@@ -416,6 +420,8 @@
             @pl.when(jnp.logical_and(has_x[a], has_y[b]))
             def _():
                 corner(a, b).wait_send()
+    for store in stores:
+        store.wait()
 
 
 def local(curve_size, groups, field, source, mass, interp, parent_list, child_list, child_kind, counts):
@@ -427,16 +433,16 @@
     mem = comps * slots
     f32 = jnp.float32
     hbm = pl.BlockSpec(memory_space=pltpu.HBM)
-    vmem = pl.BlockSpec(memory_space=pltpu.VMEM)
     dma = pltpu.SemaphoreType.DMA
     out = pl.pallas_call(
         functools.partial(kernel, curve_size, groups, rows_x, rows_y, nodes, slots, kinds, comps),
         out_shape=jax.ShapeDtypeStruct((comps, blocks, nodes), f32),
         in_specs=[hbm] * 8,
-        out_specs=vmem,
+        out_specs=hbm,
         scratch_shapes=[
             pltpu.VMEM((comps, deep, nodes), f32),
             pltpu.VMEM((comps, deep, nodes), f32),
+            pltpu.VMEM((comps, blocks, nodes), f32),
             pltpu.VMEM((comps, deep, nodes), f32),
             pltpu.VMEM((deep, nodes), f32),
             pltpu.VMEM((comps, deep, nodes), f32),
@@ -463,6 +469,7 @@
             pltpu.VMEM(child_list.shape, jnp.int32),
             pltpu.VMEM(child_kind.shape, jnp.int32),
             dma((10,)),
+            dma((rows_x // 4 if rows_x % 4 == 0 else rows_x,)),
             dma((14,)),
             dma((14,)),
             dma((groups,)),

time: 17.4 us -> 17.4 us (level)
  no operation moved by 1% of the time
where the time goes in v3:
time: 17.4 us; the launch traced here: 17.2 us
  Pallas kernels  15.2 us (87%)
  local copies, waits for them, and re-layouts  2.06 us (12%)
    pallas_call x1, Pallas kernels, local(): pl.pallas_call(functools.partial(kernel, curve_size, groups, rows_x, rows...  15.2 us
    unnamed x1, local copies, waits for them, and re-layouts  2.06 us

profile of v3, /device:TPU:0, one launch (start us, length us, event | category | flops | bytes accessed | tf_op | source)
XLA Modules:
  0.0 17.2 jit_solution(8186788448414786329)
XLA Ops:
  0.0 15.2 %shard_map.82 = f32[3,512,128]{2,1,0:T(8,128)} custom-call(f32[3,512,128]{2,1,0:T(8,128)} %bitcast.6, f32[3,512,128]{2,1,0:T(8,128)} %bitcast.7, f32[512,128]{1,0:T(8,128)} %bitcast.8, f32[512,128]{1,0:T(8,128)} %bitcast.9, s32[1,1,2,16]{3,2,1,0:T(2,128)} %parent_list.1, s32[1,1,2,16]{3,2,1,0:T(2,128)} %child_list.1, s32[1,1,2,16]{3,2,1,0:T(2,128)} %child_kind.1, ...), custom_call_target="tpu_custom_call" | custom-call | tf_op jit(solution)/shard_map/pallas_call | solution.py:437
  15.2 2.1 %copy.10 = f32[3,16,32,128]{3,2,1,0:T(8,128)} copy(f32[3,16,32,128]{3,2,1,0:T(8,128)} %bitcast.5) | data formatting | bytes 1572864
